TPU v7x, 32 devices: a whole 2x2x4 slice. The times are simulated.
32 devices in a mesh: row: 8 (over y, x, core), col: 4 (over z).
Axes of the slice: x: 2, y: 2, z: 4, core: 2. Of those that a mesh axis runs over, the one named last changes fastest.
Arguments:
- inputs: bfloat16 [1024, 14848], P('col', 'row'), may hold values from -6 to 6
- cotangent: bfloat16 [1024, 30720], P('col', 'row'), may hold values from -0.29882812 to 0.29882812
- weight: bfloat16 [14848, 30720], P('col', 'row'), may hold values from -0.046875 to 0.046875
- adapter_down_factor: bfloat16 [14848, 16], replicated, may hold values from -0.046875 to 0.046875
- adapter_up_factor: bfloat16 [16, 30720], replicated, may hold values from -1.5 to 1.5
Outputs:
- grad_input: bfloat16 [1024, 14848], P('row', 'col')
- grad_a: float32 [14848, 16], P('row')
- grad_b: float32 [16, 30720], P(None, 'row')
All inputs are finite; a program needn't handle non-finite values.
Results may differ from a plain program's by a relative error of at most 0.001.
Values may be sent and summed in bfloat16 or wider, within the bound.
A program may use at most 128 MiB of HBM per device.

v0:
```python
import jax
import jax.numpy as jnp
from jax import lax
from jax.sharding import PartitionSpec as P

scaling = 2.0


def contract_trailing_axis(left, right):
    return jnp.dot(left, right.T, preferred_element_type=jnp.float32)


def partial_rows(block_rows, weight, up_weight_slice, down_slice):
    partial_value = contract_trailing_axis(block_rows, weight)
    low_rank = contract_trailing_axis(block_rows, up_weight_slice)
    return partial_value + scaling * jnp.dot(
        low_rank, down_slice.astype(jnp.float32).T, precision=lax.Precision.HIGHEST
    )


def on_device(inputs, cotangent, weight, adapter_down_factor, adapter_up_factor):
    row_position = lax.axis_index("row")
    column_position = lax.axis_index("col")
    width_row_block = inputs.shape[1]
    width_columns = weight.shape[0]
    hidden_columns = cotangent.shape[1]
    down_factor_rows = lax.dynamic_slice_in_dim(
        adapter_down_factor, row_position * width_row_block, width_row_block, 0
    )
    down_factor_columns = lax.dynamic_slice_in_dim(
        adapter_down_factor, column_position * width_columns, width_columns, 0
    )
    up_weight_slice = lax.dynamic_slice_in_dim(
        adapter_up_factor, row_position * hidden_columns, hidden_columns, 1
    )
    low_part = contract_trailing_axis(cotangent, up_weight_slice)
    proj_part = jnp.dot(inputs, down_factor_rows, preferred_element_type=jnp.float32)
    gradient_lowrank, projected_rows = lax.psum((low_part, proj_part), "row")
    gathered = lax.all_gather(cotangent, "col", axis=0, tiled=True)
    summed = lax.psum_scatter(
        partial_rows(gathered, weight, up_weight_slice, down_factor_columns),
        "row",
        scatter_dimension=0,
        tiled=True,
    )
    grad_input = summed.astype(jnp.bfloat16)
    part_a = scaling * jnp.dot(
        inputs.astype(jnp.float32).T, gradient_lowrank, precision=lax.Precision.HIGHEST
    )
    part_b = scaling * jnp.dot(
        projected_rows.T, cotangent.astype(jnp.float32), precision=lax.Precision.HIGHEST
    )
    grad_a, grad_b = lax.psum((part_a, part_b), "col")
    return (grad_input, grad_a, grad_b)


def solution(mesh):
    in_specs = (P("col", "row"), P("col", "row"), P("col", "row"), P(), P())
    out_specs = (P("row", "col"), P("row", None), P(None, "row"))
    return jax.shard_map(
        on_device, mesh=mesh, in_specs=in_specs, out_specs=out_specs, check_vma=False
    )
```

profile of v0, /device:TPU:25, one launch (start us, length us, event | category | flops | bytes accessed | tf_op | source)
XLA Modules:
  0.0 360.0 jit_solution(3675591982956781096)
XLA Ops:
  7.2 0.0 copy-start
  7.2 0.0 all-gather.2.cloned.1.call-start
  7.2 0.7 all-gather.2.cloned.1.call-update
  7.9 0.0 reduce-scatter.2.cloned.1.call-start
  8.0 140.9 %all-gather.2.cloned.1.call-done = bf16[1024,3840]{1,0:T(8,128)(2,1)} async-done(((bf16[256,3840]{1,0:T(8,128)(2,1)}), bf16[1024,3840]{1,0:T(8,128)(2,1)}) %all-gather.2.cloned.1.call-update) | async-done | bytes 7864336 | tf_op jit(solution)/shard_map/all_gather | solution.py:39
  148.9 39.8 %fusion.10 = f32[1024,3712]{1,0:T(8,128)S(1)} fusion(bf16[1024,3840]{1,0:T(8,128)(2,1)} %all-gather.2.cloned.1.call-done, bf16[3712,3840]{1,0:T(8,128)(2,1)} %param.7), kind=kOutput, calls=%fused_computation.15 | convolution fusion | flops 29192355840 | bytes 51576832 | tf_op jit(solution)/shard_map/dot_general | solution.py:10
  188.7 0.0 copy-done
  188.7 5.4 %fusion.3 = f32[16,1024]{1,0:T(8,128)S(1)} fusion(bf16[1024,3840]{1,0:T(8,128)(2,1)} %all-gather.2.cloned.1.call-done, bf16[16,30720]{1,0:T(8,128)(2,1)S(1)} %copy-done, s32[]{:T(128)S(6)} %select_n.9), kind=kOutput, calls=%fused_computation.8 | convolution fusion | flops 125829120 | bytes 8052740 | tf_op jit(solution)/shard_map/dot_general | solution.py:10
  194.0 11.5 %multiply_add_fusion = f32[1024,3712]{1,0:T(8,128)} fusion(f32[1024,3712]{1,0:T(8,128)S(1)} %fusion.10, f32[16,1024]{1,0:T(8,128)S(1)} %fusion.3, bf16[14848,16]{0,1:T(8,128)(2,1)} %param.8, s32[]{:T(128)S(6)} %select_n.10), kind=kOutput, calls=%fused_computation | convolution fusion | flops 737411072 | bytes 30593028 | tf_op jit(solution)/shard_map/dot_general | solution.py:16
  205.5 0.0 copy-start.1
  205.5 0.0 reduce-scatter.2.cloned.1.call-update
  205.6 0.0 all-reduce.4.cloned.1.call-start
  205.6 1.6 convolution_bitcast_fusion
  207.2 0.2 copy-done.1
  207.4 0.6 convolution_bitcast_fusion.1
  208.0 21.8 %all-reduce = (f32[256,16]{0,1:T(8,128)S(1)}, f32[256,16]{0,1:T(8,128)S(1)}) all-reduce(f32[256,16]{0,1:T(8,128)S(1)} %convolution_bitcast_fusion.1, f32[256,16]{0,1:T(8,128)S(1)} %convolution_bitcast_fusion), channel_id=1, replica_groups=mesh['row'=8,'col'=4] {'row'}, use_global_device_ids=true, to_apply=%region_1.0 | all-reduce | flops 8192 | bytes 65536 | tf_op jit(solution)/shard_map/psum | solution.py:38
  229.8 2.8 fusion
  232.5 1.6 convolution_multiply_fusion
  234.1 0.0 all-reduce.4.cloned.1.call-update
  234.2 79.0 %reduce-scatter.2.cloned.1.call-done = f32[128,3712]{1,0:T(8,128)} async-done(((f32[1024,3712]{1,0:T(8,128)}), f32[128,3712]{1,0:T(8,128)}) %reduce-scatter.2.cloned.1.call-update) | async-done | bytes 1900560 | tf_op jit(solution)/shard_map/reduce_scatter | solution.py:40
  313.1 2.6 convert_element_type.2
  315.7 34.6 %all-reduce.4.cloned.1.call-done = (f32[1856,16]{0,1:T(8,128)}, f32[16,3840]{1,0:T(8,128)}) async-done(((f32[1856,16]{0,1:T(8,128)}, f32[16,3840]{1,0:T(8,128)}), (f32[1856,16]{0,1:T(8,128)}, f32[16,3840]{1,0:T(8,128)})) %all-reduce.4.cloned.1.call-update) | async-done | bytes 364560 | tf_op jit(solution)/shard_map/psum | solution.py:53
  350.3 1.6 copy.10
  351.8 1.7 copy.11
Async XLA Ops:
  7.2 181.5 %copy-start = (bf16[16,30720]{1,0:T(8,128)(2,1)S(1)}, bf16[16,30720]{1,0:T(8,128)(2,1)}, u32[]{:S(2)}) copy-start(bf16[16,30720]{1,0:T(8,128)(2,1)} %param.9) | copy-start | bytes 2949124
  7.2 141.7 %all-gather.2.cloned.1.call-start = ((), (), s32[]{:S(2)}) async-start(), calls=%async_computation.1 | async-start | bytes 9830400 | tf_op jit(solution)/shard_map/all_gather | solution.py:39
  7.9 305.2 %reduce-scatter.2.cloned.1.call-start = ((), (), s32[]{:S(2)}) async-start(), calls=%async_computation.2 | async-start | bytes 17104896 | tf_op jit(solution)/shard_map/reduce_scatter | solution.py:40
  205.5 1.9 copy-start.1
  205.6 144.7 %all-reduce.4.cloned.1.call-start = ((), (), s32[]{:S(2)}) async-start(), calls=%async_computation.3 | async-start | bytes 737280 | tf_op jit(solution)/shard_map/psum | solution.py:53
Sparse Core Ops, SparseCore 0:
  9.6 139.2 all-gather.1
  205.7 107.3 reduce-scatter.1
  316.1 34.1 all-reduce.3
where the time goes:
time: 364 us; the launch traced here: 360 us
  waiting for transfers between devices  255 us (70%)
  matrix products  63.2 us (17%)
  blocking collectives  21.8 us (6%)
  between operations  13.8 us (4%)
    all_gather x1, waiting for transfers between devices, on_device(): gathered = lax.all_gather(cotangent, 'col', axis=0, tiled=True)  141 us
    reduce_scatter x1, waiting for transfers between devices, on_device(): lax.psum_scatter(partial_rows(gathered, weight, up_weight_slice, down_fac...  79 us
    dot_general x3, matrix products, contract_trailing_axis(): return jnp.dot(left, right.T, preferred_element_type=jnp.float32)  45.8 us
    psum x1, waiting for transfers between devices, on_device(): grad_a, grad_b = lax.psum((part_a, part_b), 'col')  34.6 us
    psum x1, blocking collectives, on_device(): gradient_lowrank, projected_rows = lax.psum((low_part, proj_part), 'row')  21.8 us
    dot_general x1, matrix products, partial_rows(): jnp.dot(low_rank, down_slice.astype(jnp.float32).T, precision=lax.Precisi...  11.5 us
  transfers between devices with their start and end apart: 3, of which 3 were waited for; matrix products, arithmetic and copies ran while one was open for 3% of the time, Pallas kernels for 0%

commit v1 on v0

v1 whole, which is shorter than its diff:
```python
import functools

import jax
import jax.numpy as jnp
from jax import lax
from jax.experimental import pallas as pl
from jax.experimental.pallas import tpu as pltpu
from jax.sharding import PartitionSpec as P

scaling = 2.0
MESH = pl.DeviceIdType.MESH
CHUNK = 64
SLOTS = 4


def contract_trailing_axis(left, right):
    return lax.dot_general(
        left, right, (((1,), (1,)), ((), ())), preferred_element_type=jnp.float32
    )


def input_gradient_kernel(
    n, rows, cot_hbm, weight_hbm, up3, down3, out,
    gathered, weight, part, core_in, half, arrive, fin,
    load_sem, zsend, zrecv, core_send, core_recv, quarter_send, arrive_sem,
    fin_send, fin_recv, credit,
):
    z = lax.axis_index("col")
    r = lax.axis_index("row")
    core = r % 2
    x = (r // 2) % 2
    y = r // 4
    ny = rows // 4
    shard = cot_hbm.shape[0]
    width = weight_hbm.shape[0]
    m = CHUNK
    chunks = shard // m
    total = n * chunks
    own_rows = out.shape[0]
    h2, h4 = m // 2, m // 4
    partner = {"row": r + 1 - 2 * core}
    x_peer = {"row": y * 4 + (1 - x) * 2 + core}

    def y_peer(step):
        return {"row": ((y + step) % ny) * 4 + x * 2 + core}

    load_weight = pltpu.make_async_copy(weight_hbm, weight, load_sem.at[0])
    load_own = pltpu.make_async_copy(
        cot_hbm, gathered.at[pl.ds(pl.multiple_of(z * shard, 16), shard)], load_sem.at[1]
    )
    load_own.start()
    load_weight.start()

    barrier = pltpu.get_barrier_semaphore()
    peers = [partner, x_peer] + [y_peer(k) for k in range(1, ny)]
    for peer in peers:
        pl.semaphore_signal(barrier, inc=1, device_id=peer, device_id_type=MESH)

    @pl.when(z > 0)
    def _():
        pl.semaphore_signal(barrier, inc=1, device_id={"col": z - 1}, device_id_type=MESH)

    @pl.when(z < n - 1)
    def _():
        pl.semaphore_signal(barrier, inc=1, device_id={"col": z + 1}, device_id_type=MESH)

    ends = jnp.where(z > 0, 1, 0) + jnp.where(z < n - 1, 1, 0)
    pl.semaphore_wait(barrier, len(peers) + ends)
    load_own.wait()

    def rows_of(s, c):
        return pl.ds(pl.multiple_of(s * shard + c * m, 16), m)

    def z_copy(s, c, side, target):
        block = gathered.at[rows_of(s, c)]
        return pltpu.make_async_remote_copy(
            src_ref=block,
            dst_ref=block,
            send_sem=zsend.at[side, s * chunks + c],
            recv_sem=zrecv.at[s * chunks + c],
            device_id={"col": target},
            device_id_type=MESH,
        )

    def pass_left(s, c):
        @pl.when(z > 0)
        def _():
            z_copy(s, c, 0, z - 1).start()

    def pass_right(s, c):
        @pl.when(z < n - 1)
        def _():
            z_copy(s, c, 1, z + 1).start()

    pass_left(z, 0)
    pass_right(z, 0)

    pairs = jnp.minimum(z, n - 1 - z)

    def place(i):
        c, p = i // n, i % n
        near = (p + 1) // 2
        near_shard = jnp.where(p % 2 == 1, z + near, z - near)
        far = p - pairs
        far_shard = jnp.where(z < n - 1 - z, z + far, z - far)
        s = jnp.where(p <= 2 * pairs, near_shard, far_shard)
        token = s * shard + c * m
        dest = token // own_rows
        return c, p, s, dest, token % own_rows

    def copy_core(slot):
        return pltpu.make_async_remote_copy(
            src_ref=part.at[pl.ds(pl.multiple_of((1 - core) * h2, 8), h2)],
            dst_ref=core_in.at[slot],
            send_sem=core_send.at[slot],
            recv_sem=core_recv.at[slot],
            device_id=partner,
            device_id_type=MESH,
        )

    def copy_quarter(slot, q, landing, target):
        return pltpu.make_async_remote_copy(
            src_ref=half.at[slot, pl.ds(q * h4, h4)],
            dst_ref=arrive.at[slot, landing],
            send_sem=quarter_send.at[slot, q],
            recv_sem=arrive_sem.at[slot, landing],
            device_id=target,
            device_id_type=MESH,
        )

    def first_hop(slot, dest):
        yd, xd = dest // 4, (dest // 2) % 2

        @pl.when(y != yd)
        def _():
            landing = 2 + (y - yd + ny) % ny - 1
            copy_quarter(slot, 0, landing, {"row": yd * 4 + x * 2 + core}).start()

        @pl.when(x != xd)
        def _():
            copy_quarter(slot, 1, 0, x_peer).start()

    def wait_landing(slot, landing):
        copy_quarter(slot, 0, landing, x_peer).wait_recv()

    def second_hop(i):
        _, _, _, dest, _ = place(i)
        slot = i % SLOTS
        yd, xd = dest // 4, (dest // 2) % 2

        @pl.when(y == yd)
        def _():
            for k in range(ny - 1):
                wait_landing(slot, 2 + k)
                half[slot, pl.ds(0, h4)] += arrive[slot, 2 + k]

            @pl.when(x != xd)
            def _():
                copy_quarter(slot, 0, 1, x_peer).start()

        @pl.when(x == xd)
        def _():
            wait_landing(slot, 0)
            half[slot, pl.ds(h4, h4)] += arrive[slot, 0]

            @pl.when(y != yd)
            def _():
                landing = 2 + ny - 1 + (y - yd + ny) % ny - 1
                copy_quarter(slot, 1, landing, {"row": yd * 4 + x * 2 + core}).start()

    def fin_copy(start, index):
        return pltpu.make_async_remote_copy(
            src_ref=fin,
            dst_ref=out.at[pl.ds(pl.multiple_of(start, 16), h2)],
            send_sem=fin_send.at[0],
            recv_sem=fin_recv.at[index],
            device_id=partner,
            device_id_type=MESH,
        )

    def finish(i):
        _, _, _, dest, local = place(i)
        slot = i % SLOTS
        yd, xd, cored = dest // 4, (dest // 2) % 2, dest % 2
        here = jnp.logical_and(y == yd, x == xd)

        @pl.when(here)
        def _():
            wait_landing(slot, 1)
            half[slot, pl.ds(0, h4)] += arrive[slot, 1]
            for k in range(ny - 1):
                wait_landing(slot, 2 + ny - 1 + k)
                half[slot, pl.ds(h4, h4)] += arrive[slot, 2 + ny - 1 + k]
            start = local + core * h2

            @pl.when(core == cored)
            def _():
                out[pl.ds(pl.multiple_of(start, 16), h2)] = half[slot].astype(jnp.bfloat16)

            @pl.when(core != cored)
            def _():
                fin[...] = half[slot].astype(jnp.bfloat16)
                copy = fin_copy(start, local // m)
                copy.start()
                copy.wait_send()

        @pl.when(jnp.logical_not(here))
        def _():
            copy_quarter(slot, 0, 0, x_peer).wait_send()
            copy_quarter(slot, 1, 0, x_peer).wait_send()

        @pl.when(i < total - SLOTS)
        def _():
            for k, peer in enumerate(peers):
                index = k if k < 2 else 2 + (ny - (k - 1)) - 1
                pl.semaphore_signal(credit.at[index], inc=1, device_id=peer, device_id_type=MESH)

    block = min(256, width)
    whole_blocks = width // block

    def multiply(block_rows, low):
        def columns(start, size):
            value = contract_trailing_axis(block_rows, weight[pl.ds(start, size)])
            part[:, pl.ds(start, size)] = value + contract_trailing_axis(
                low, down3[pl.ds(start, size)]
            )

        @pl.loop(0, whole_blocks)
        def _(j):
            columns(pl.multiple_of(j * block, block), block)

        if width % block:
            columns(whole_blocks * block, width % block)

    @pl.loop(0, total)
    def _(i):
        c, p, s, dest, _ = place(i)
        slot = i % SLOTS

        @pl.when(jnp.logical_and(p == 0, c + 1 < chunks))
        def _():
            pass_left(z, c + 1)
            pass_right(z, c + 1)

        @pl.when(s != z)
        def _():
            z_copy(s, c, 0, z).wait_recv()

        @pl.when(s > z)
        def _():
            pass_left(s, c)

        @pl.when(s < z)
        def _():
            pass_right(s, c)

        @pl.when(i == 0)
        def _():
            load_weight.wait()

        block_rows = gathered[rows_of(s, c)]
        rank3 = up3.shape[0]
        rank = rank3 // 3
        low = contract_trailing_axis(block_rows, up3[...])
        high = low.astype(jnp.bfloat16)
        rest = low - high.astype(jnp.float32)
        middle = rest.astype(jnp.bfloat16)
        last = (rest - middle.astype(jnp.float32)).astype(jnp.bfloat16)
        lane = lax.broadcasted_iota(jnp.int32, low.shape, 1)
        split = jnp.where(
            lane < rank,
            high.astype(jnp.float32),
            jnp.where(lane < 2 * rank, middle.astype(jnp.float32), last.astype(jnp.float32)),
        ).astype(jnp.bfloat16)
        multiply(block_rows, split)

        @pl.when(i >= SLOTS)
        def _():
            for k in range(len(peers)):
                pl.semaphore_wait(credit.at[k], 1)

        exchange = copy_core(slot)
        exchange.start()
        exchange.wait()
        half[slot] = part[pl.ds(pl.multiple_of(core * h2, 8), h2)] + core_in[slot]
        first_hop(slot, dest)

        @pl.when(i >= 1)
        def _():
            second_hop(i - 1)

        @pl.when(i >= 2)
        def _():
            finish(i - 2)

    second_hop(total - 1)
    finish(total - 2)
    finish(total - 1)

    for index in range(own_rows // m):
        fin_copy(index * m, index).wait_recv()

    @pl.loop(0, total)
    def _(i):
        c, _, s, _, _ = place(i)

        @pl.when(jnp.logical_and(z > 0, s >= z))
        def _():
            z_copy(s, c, 0, z).wait_send()

        @pl.when(jnp.logical_and(z < n - 1, s <= z))
        def _():
            z_copy(s, c, 1, z).wait_send()


def input_gradient(n, rows, cotangent, weight, up_slice, down_slice):
    shard, hidden = cotangent.shape
    width = weight.shape[0]
    tokens = shard * n
    m = CHUNK
    total = tokens // m
    ny = rows // 4
    own_rows = tokens // rows
    up3 = jnp.concatenate([up_slice] * 3, axis=0)
    down3 = jnp.concatenate([down_slice * jnp.bfloat16(scaling)] * 3, axis=1)
    vmem = pl.BlockSpec(memory_space=pltpu.VMEM)
    hbm = pl.BlockSpec(memory_space=pl.ANY)
    return pl.pallas_call(
        functools.partial(input_gradient_kernel, n, rows),
        out_shape=jax.ShapeDtypeStruct((own_rows, width), jnp.bfloat16),
        in_specs=[hbm, hbm, vmem, vmem],
        out_specs=vmem,
        scratch_shapes=[
            pltpu.VMEM((tokens, hidden), jnp.bfloat16),
            pltpu.VMEM((width, hidden), jnp.bfloat16),
            pltpu.VMEM((m, width), jnp.float32),
            pltpu.VMEM((SLOTS, m // 2, width), jnp.float32),
            pltpu.VMEM((SLOTS, m // 2, width), jnp.float32),
            pltpu.VMEM((SLOTS, 2 * ny, m // 4, width), jnp.float32),
            pltpu.VMEM((m // 2, width), jnp.bfloat16),
            pltpu.SemaphoreType.DMA((2,)),
            pltpu.SemaphoreType.DMA((2, total)),
            pltpu.SemaphoreType.DMA((total,)),
            pltpu.SemaphoreType.DMA((SLOTS,)),
            pltpu.SemaphoreType.DMA((SLOTS,)),
            pltpu.SemaphoreType.DMA((SLOTS, 2)),
            pltpu.SemaphoreType.DMA((SLOTS, 2 * ny)),
            pltpu.SemaphoreType.DMA((1,)),
            pltpu.SemaphoreType.DMA((own_rows // m,)),
            pltpu.SemaphoreType.REGULAR((ny + 1,)),
        ],
        compiler_params=pltpu.CompilerParams(
            collective_id=0, has_side_effects=True, vmem_limit_bytes=62 * 2**20
        ),
        cost_estimate=pl.CostEstimate(
            flops=2 * tokens * width * hidden,
            bytes_accessed=2 * width * hidden,
            transcendentals=0,
        ),
        name="input_gradient",
    )(cotangent, weight, up3, down3)


def on_device(n, rows, inputs, cotangent, weight, adapter_down_factor, adapter_up_factor):
    row_position = lax.axis_index("row")
    column_position = lax.axis_index("col")
    width_row_block = inputs.shape[1]
    width_columns = weight.shape[0]
    hidden_columns = cotangent.shape[1]
    down_factor_rows = lax.dynamic_slice_in_dim(
        adapter_down_factor, row_position * width_row_block, width_row_block, 0
    )
    down_factor_columns = lax.dynamic_slice_in_dim(
        adapter_down_factor, column_position * width_columns, width_columns, 0
    )
    up_weight_slice = lax.dynamic_slice_in_dim(
        adapter_up_factor, row_position * hidden_columns, hidden_columns, 1
    )
    grad_input = input_gradient(
        n, rows, cotangent, weight, up_weight_slice, down_factor_columns
    )
    low_part = contract_trailing_axis(cotangent, up_weight_slice)
    proj_part = jnp.dot(inputs, down_factor_rows, preferred_element_type=jnp.float32)
    gradient_lowrank, projected_rows = lax.psum((low_part, proj_part), "row")
    part_a = scaling * jnp.dot(
        inputs.astype(jnp.float32).T, gradient_lowrank, precision=lax.Precision.HIGHEST
    )
    part_b = scaling * jnp.dot(
        projected_rows.T, cotangent.astype(jnp.float32), precision=lax.Precision.HIGHEST
    )
    grad_a, grad_b = lax.psum((part_a, part_b), "col")
    return (grad_input, grad_a, grad_b)


def solution(mesh):
    in_specs = (P("col", "row"), P("col", "row"), P("col", "row"), P(), P())
    out_specs = (P("row", "col"), P("row", None), P(None, "row"))
    body = functools.partial(on_device, mesh.shape["col"], mesh.shape["row"])
    return jax.shard_map(
        body, mesh=mesh, in_specs=in_specs, out_specs=out_specs, check_vma=False
    )
```

time: 364 us -> 298 us (0.82); the launches traced: 360 us -> 298 us
  waiting for transfers between devices: 255 us -> 0.04 us
  Pallas kernels: 0 us -> 246 us
  matrix products: 63.2 us -> 8.11 us
    pallas_call x0 -> x1, Pallas kernels: none -> 246 us  [input_gradient(): pl.pallas_call(functools.partial(input_gradient_kernel, n, rows), out_sha...]
    all_gather x1 -> x0, waiting for transfers between devices: 141 us -> none  [on_device(): gathered = lax.all_gather(cotangent, 'col', axis=0, tiled=True)]
    reduce_scatter x1 -> x0, waiting for transfers between devices: 79 us -> none  [on_device(): lax.psum_scatter(partial_rows(gathered, weight, up_weight_slice, down_fac...]
    dot_general x4 -> x1, matrix products: 57.2 us -> 2.27 us  [contract_trailing_axis(): lax.dot_general(left, right, (((1,), (1,)), ((), ())), preferred_element_...]
    psum x1, waiting for transfers between devices: 34.6 us -> 0.02 us  [on_device(): grad_a, grad_b = lax.psum((part_a, part_b), 'col')]
  transfers between devices with their start and end apart: 3 -> 1, of which waited for: 3 -> 0; matrix products, arithmetic and copies ran while one was open for 3% -> 1% of each run, Pallas kernels for 0% -> 83%
where the time goes in v1:
time: 298 us
  Pallas kernels  246 us (83%)
  blocking collectives  21.6 us (7%)
  between operations  14.1 us (5%)
  matrix products  8.11 us (3%)
  local copies, waits for them, and re-layouts  6.04 us (2%)
    pallas_call x1, Pallas kernels, input_gradient(): pl.pallas_call(functools.partial(input_gradient_kernel, n, rows), out_sha...  246 us
    psum x1, blocking collectives, on_device(): gradient_lowrank, projected_rows = lax.psum((low_part, proj_part), 'row')  21.6 us
  transfers between devices with their start and end apart: 1, of which 0 were waited for; matrix products, arithmetic and copies ran while one was open for 1% of the time, Pallas kernels for 83%

profile of v1, /device:TPU:25, one launch (start us, length us, event | category | flops | bytes accessed | tf_op | source)
XLA Modules:
  0.0 297.8 jit_solution(14156550033038310963)
XLA Ops:
  7.2 0.0 copy-start
  7.2 0.0 all-reduce.4.cloned.1.call-start
  7.2 1.1 copy-done
  8.4 0.0 copy-start.1
  8.4 2.3 convolution_bitcast_fusion.1
  10.7 1.6 convolution_bitcast_fusion
  12.2 21.6 %all-reduce = (f32[256,16]{0,1:T(8,128)S(1)}, f32[256,16]{0,1:T(8,128)S(1)}) all-reduce(f32[256,16]{0,1:T(8,128)S(1)} %convolution_bitcast_fusion.1, f32[256,16]{0,1:T(8,128)S(1)} %convolution_bitcast_fusion), channel_id=1, replica_groups=mesh['row'=8,'col'=4] {'row'}, use_global_device_ids=true, to_apply=%region_0.0 | all-reduce | flops 8192 | bytes 65536 | tf_op jit(solution)/shard_map/psum | solution.py:384
  33.8 2.7 fusion
  36.5 0.0 copy-done.1
  36.5 1.6 convolution_multiply_fusion
  38.1 0.0 all-reduce.4.cloned.1.call-update
  38.1 0.8 pad_maximum_fusion.up3
  38.9 0.9 dynamic-slice_multiply_fusion
  39.8 1.3 copy.9.down3
  41.1 246.2 %input_gradient.1 = bf16[128,3712]{1,0:T(8,128)(2,1)} custom-call(bf16[256,3840]{1,0:T(8,128)(2,1)} %cot_hbm.1, bf16[3712,3840]{1,0:T(8,128)(2,1)} %weight_hbm.1, bf16[48,3840]{1,0:T(8,128)(2,1)} %pad_maximum_fusion.up3, bf16[3712,48]{1,0:T(8,128)(2,1)} %copy.9.down3), custom_call_target="tpu_custom_call" | custom-call | flops 29192355840 | bytes 28508160 | tf_op jit(solution)/shard_map/input_gradient/pallas_call | solution.py:328
  287.4 0.0 all-reduce.4.cloned.1.call-done
  287.4 0.0 copy-start.3
  287.4 0.0 copy-start.2
  287.4 2.2 copy.13
  289.6 0.0 copy-done.3
  289.7 0.6 copy.14
  290.3 0.0 copy-done.2
  290.3 0.7 copy.15
  (2 shorter events, 0.0 us)
Async XLA Ops:
  7.2 1.2 copy-start
  7.2 280.2 %all-reduce.4.cloned.1.call-start = ((), (), s32[]{:S(2)}) async-start(), calls=%async_computation | async-start | bytes 737280 | tf_op jit(solution)/shard_map/psum | solution.py:391
  8.4 28.1 %copy-start.1 = (bf16[256,3840]{1,0:T(8,128)(2,1)S(1)}, bf16[256,3840]{1,0:T(8,128)(2,1)}, u32[]{:S(2)}) copy-start(bf16[256,3840]{1,0:T(8,128)(2,1)} %cot_hbm.1) | copy-start | bytes 5898244
  287.4 2.3 copy-start.3
  287.4 2.9 copy-start.2
Sparse Core Ops, SparseCore 0:
  38.2 42.4 all-reduce.3

commit v2 on v1

--- a/solution.py
+++ b/solution.py
@@ -10,7 +10,6 @@
 scaling = 2.0
 MESH = pl.DeviceIdType.MESH
 CHUNK = 64
-SLOTS = 4
 
 
 def contract_trailing_axis(left, right):
@@ -20,7 +19,7 @@
 
 
 def input_gradient_kernel(
-    n, rows, cot_hbm, weight_hbm, up3, down3, out,
+    n, rows, batches, cot_hbm, weight_hbm, up3, down3, out,
     gathered, weight, part, core_in, half, arrive, fin,
     load_sem, zsend, zrecv, core_send, core_recv, quarter_send, arrive_sem,
     fin_send, fin_recv, credit,
@@ -38,6 +37,7 @@
     total = n * chunks
     own_rows = out.shape[0]
     h2, h4 = m // 2, m // 4
+    slots = half.shape[0]
     partner = {"row": r + 1 - 2 * core}
     x_peer = {"row": y * 4 + (1 - x) * 2 + core}
 
@@ -46,7 +46,7 @@
 
     load_weight = pltpu.make_async_copy(weight_hbm, weight, load_sem.at[0])
     load_own = pltpu.make_async_copy(
-        cot_hbm, gathered.at[pl.ds(pl.multiple_of(z * shard, 16), shard)], load_sem.at[1]
+        cot_hbm, gathered.at[pl.ds(0, shard)], load_sem.at[1]
     )
     load_own.start()
     load_weight.start()
@@ -68,14 +68,20 @@
     pl.semaphore_wait(barrier, len(peers) + ends)
     load_own.wait()
 
-    def rows_of(s, c):
-        return pl.ds(pl.multiple_of(s * shard + c * m, 16), m)
+    def position(holder, s, c):
+        pairs = jnp.minimum(holder, n - 1 - holder)
+        distance = jnp.where(s > holder, s - holder, holder - s)
+        near = jnp.where(s > holder, 2 * distance - 1, 2 * distance)
+        p = jnp.where(distance <= pairs, near, pairs + distance)
+        return jnp.where(s == holder, c, chunks + c * (n - 1) + p - 1)
+
+    def rows_at(i):
+        return pl.ds(pl.multiple_of(i * m, 16), m)
 
     def z_copy(s, c, side, target):
-        block = gathered.at[rows_of(s, c)]
         return pltpu.make_async_remote_copy(
-            src_ref=block,
-            dst_ref=block,
+            src_ref=gathered.at[rows_at(position(z, s, c))],
+            dst_ref=gathered.at[rows_at(position(target, s, c))],
             send_sem=zsend.at[side, s * chunks + c],
             recv_sem=zrecv.at[s * chunks + c],
             device_id={"col": target},
@@ -92,13 +98,17 @@
         def _():
             z_copy(s, c, 1, z + 1).start()
 
-    pass_left(z, 0)
-    pass_right(z, 0)
+    ahead = min(2, chunks)
+    for c in range(ahead):
+        pass_left(z, c)
+        pass_right(z, c)
 
     pairs = jnp.minimum(z, n - 1 - z)
 
     def place(i):
-        c, p = i // n, i % n
+        q = jnp.maximum(i - chunks, 0)
+        c = jnp.where(i < chunks, i, q // (n - 1))
+        p = jnp.where(i < chunks, 0, q % (n - 1) + 1)
         near = (p + 1) // 2
         near_shard = jnp.where(p % 2 == 1, z + near, z - near)
         far = p - pairs
@@ -108,9 +118,9 @@
         dest = token // own_rows
         return c, p, s, dest, token % own_rows
 
-    def copy_core(slot):
+    def copy_core(slot, row):
         return pltpu.make_async_remote_copy(
-            src_ref=part.at[pl.ds(pl.multiple_of((1 - core) * h2, 8), h2)],
+            src_ref=part.at[pl.ds(pl.multiple_of(row + (1 - core) * h2, 8), h2)],
             dst_ref=core_in.at[slot],
             send_sem=core_send.at[slot],
             recv_sem=core_recv.at[slot],
@@ -145,7 +155,7 @@
 
     def second_hop(i):
         _, _, _, dest, _ = place(i)
-        slot = i % SLOTS
+        slot = i % slots
         yd, xd = dest // 4, (dest // 2) % 2
 
         @pl.when(y == yd)
@@ -180,7 +190,7 @@
 
     def finish(i):
         _, _, _, dest, local = place(i)
-        slot = i % SLOTS
+        slot = i % slots
         yd, xd, cored = dest // 4, (dest // 2) % 2, dest % 2
         here = jnp.logical_and(y == yd, x == xd)
 
@@ -209,7 +219,7 @@
             copy_quarter(slot, 0, 0, x_peer).wait_send()
             copy_quarter(slot, 1, 0, x_peer).wait_send()
 
-        @pl.when(i < total - SLOTS)
+        @pl.when(i < total - slots)
         def _():
             for k, peer in enumerate(peers):
                 index = k if k < 2 else 2 + (ny - (k - 1)) - 1
@@ -218,50 +228,11 @@
     block = min(256, width)
     whole_blocks = width // block
 
-    def multiply(block_rows, low):
-        def columns(start, size):
-            value = contract_trailing_axis(block_rows, weight[pl.ds(start, size)])
-            part[:, pl.ds(start, size)] = value + contract_trailing_axis(
-                low, down3[pl.ds(start, size)]
-            )
-
-        @pl.loop(0, whole_blocks)
-        def _(j):
-            columns(pl.multiple_of(j * block, block), block)
-
-        if width % block:
-            columns(whole_blocks * block, width % block)
-
-    @pl.loop(0, total)
-    def _(i):
-        c, p, s, dest, _ = place(i)
-        slot = i % SLOTS
-
-        @pl.when(jnp.logical_and(p == 0, c + 1 < chunks))
-        def _():
-            pass_left(z, c + 1)
-            pass_right(z, c + 1)
-
-        @pl.when(s != z)
-        def _():
-            z_copy(s, c, 0, z).wait_recv()
-
-        @pl.when(s > z)
-        def _():
-            pass_left(s, c)
-
-        @pl.when(s < z)
-        def _():
-            pass_right(s, c)
-
-        @pl.when(i == 0)
-        def _():
-            load_weight.wait()
-
-        block_rows = gathered[rows_of(s, c)]
-        rank3 = up3.shape[0]
-        rank = rank3 // 3
-        low = contract_trailing_axis(block_rows, up3[...])
+    def multiply(first, count):
+        size = count * m
+        lhs = pl.ds(first * m, size)
+        rank = up3.shape[0] // 3
+        low = contract_trailing_axis(gathered[lhs], up3[...])
         high = low.astype(jnp.bfloat16)
         rest = low - high.astype(jnp.float32)
         middle = rest.astype(jnp.bfloat16)
@@ -272,30 +243,73 @@
             high.astype(jnp.float32),
             jnp.where(lane < 2 * rank, middle.astype(jnp.float32), last.astype(jnp.float32)),
         ).astype(jnp.bfloat16)
-        multiply(block_rows, split)
-
-        @pl.when(i >= SLOTS)
-        def _():
-            for k in range(len(peers)):
-                pl.semaphore_wait(credit.at[k], 1)
-
-        exchange = copy_core(slot)
-        exchange.start()
-        exchange.wait()
-        half[slot] = part[pl.ds(pl.multiple_of(core * h2, 8), h2)] + core_in[slot]
-        first_hop(slot, dest)
-
-        @pl.when(i >= 1)
-        def _():
-            second_hop(i - 1)
-
-        @pl.when(i >= 2)
-        def _():
-            finish(i - 2)
-
-    second_hop(total - 1)
-    finish(total - 2)
-    finish(total - 1)
+
+        def columns(start, extent):
+            value = contract_trailing_axis(gathered[lhs], weight[pl.ds(start, extent)])
+            part[pl.ds(0, size), pl.ds(start, extent)] = value + contract_trailing_axis(
+                split, down3[pl.ds(start, extent)]
+            )
+
+        @pl.loop(0, whole_blocks)
+        def _(j):
+            columns(pl.multiple_of(j * block, block), block)
+
+        if width % block:
+            columns(whole_blocks * block, width % block)
+
+    def receive(i):
+        c, p, s, _, _ = place(i)
+
+        @pl.when(jnp.logical_and(p == 1, c + ahead < chunks))
+        def _():
+            pass_left(z, c + ahead)
+            pass_right(z, c + ahead)
+
+        z_copy(s, c, 0, z).wait_recv()
+
+        @pl.when(s > z)
+        def _():
+            pass_left(s, c)
+
+        @pl.when(s < z)
+        def _():
+            pass_right(s, c)
+
+    previous = None
+    for first, count in batches:
+        if first >= chunks:
+            pl.loop(first, first + count)(receive)
+        if previous is not None:
+            pl.loop(previous[0], sum(previous))(second_hop)
+        if first == 0:
+            load_weight.wait()
+        multiply(first, count)
+        if previous is not None:
+            pl.loop(previous[0], sum(previous))(finish)
+
+        @pl.loop(first, first + count)
+        def _(i):
+            @pl.when(i >= slots)
+            def _():
+                for k in range(len(peers)):
+                    pl.semaphore_wait(credit.at[k], 1)
+
+            copy_core(i % slots, (i - first) * m).start()
+
+        @pl.loop(first, first + count)
+        def _(i):
+            _, _, _, dest, _ = place(i)
+            slot = i % slots
+            row = (i - first) * m
+            copy_core(slot, row).wait()
+            own = pl.ds(pl.multiple_of(row + core * h2, 8), h2)
+            half[slot] = part[own] + core_in[slot]
+            first_hop(slot, dest)
+
+        previous = (first, count)
+
+    pl.loop(previous[0], sum(previous))(second_hop)
+    pl.loop(previous[0], sum(previous))(finish)
 
     for index in range(own_rows // m):
         fin_copy(index * m, index).wait_recv()
@@ -311,6 +325,16 @@
         @pl.when(jnp.logical_and(z < n - 1, s <= z))
         def _():
             z_copy(s, c, 1, z).wait_send()
+
+
+def plan(n, chunks):
+    batches = [(0, chunks)]
+    first, end = chunks, chunks * n
+    while first < end:
+        count = n if first == chunks else n - 1
+        batches.append((first, min(count, end - first)))
+        first += count
+    return tuple(batches)
 
 
 def input_gradient(n, rows, cotangent, weight, up_slice, down_slice):
@@ -321,30 +345,32 @@
     total = tokens // m
     ny = rows // 4
     own_rows = tokens // rows
+    batches = plan(n, shard // m)
+    slots = max(count for _, count in batches)
     up3 = jnp.concatenate([up_slice] * 3, axis=0)
     down3 = jnp.concatenate([down_slice * jnp.bfloat16(scaling)] * 3, axis=1)
     vmem = pl.BlockSpec(memory_space=pltpu.VMEM)
     hbm = pl.BlockSpec(memory_space=pl.ANY)
     return pl.pallas_call(
-        functools.partial(input_gradient_kernel, n, rows),
+        functools.partial(input_gradient_kernel, n, rows, batches),
         out_shape=jax.ShapeDtypeStruct((own_rows, width), jnp.bfloat16),
         in_specs=[hbm, hbm, vmem, vmem],
         out_specs=vmem,
         scratch_shapes=[
             pltpu.VMEM((tokens, hidden), jnp.bfloat16),
             pltpu.VMEM((width, hidden), jnp.bfloat16),
-            pltpu.VMEM((m, width), jnp.float32),
-            pltpu.VMEM((SLOTS, m // 2, width), jnp.float32),
-            pltpu.VMEM((SLOTS, m // 2, width), jnp.float32),
-            pltpu.VMEM((SLOTS, 2 * ny, m // 4, width), jnp.float32),
+            pltpu.VMEM((slots * m, width), jnp.float32),
+            pltpu.VMEM((slots, m // 2, width), jnp.float32),
+            pltpu.VMEM((slots, m // 2, width), jnp.float32),
+            pltpu.VMEM((slots, 2 * ny, m // 4, width), jnp.float32),
             pltpu.VMEM((m // 2, width), jnp.bfloat16),
             pltpu.SemaphoreType.DMA((2,)),
             pltpu.SemaphoreType.DMA((2, total)),
             pltpu.SemaphoreType.DMA((total,)),
-            pltpu.SemaphoreType.DMA((SLOTS,)),
-            pltpu.SemaphoreType.DMA((SLOTS,)),
-            pltpu.SemaphoreType.DMA((SLOTS, 2)),
-            pltpu.SemaphoreType.DMA((SLOTS, 2 * ny)),
+            pltpu.SemaphoreType.DMA((slots,)),
+            pltpu.SemaphoreType.DMA((slots,)),
+            pltpu.SemaphoreType.DMA((slots, 2)),
+            pltpu.SemaphoreType.DMA((slots, 2 * ny)),
             pltpu.SemaphoreType.DMA((1,)),
             pltpu.SemaphoreType.DMA((own_rows // m,)),
             pltpu.SemaphoreType.REGULAR((ny + 1,)),

time: 298 us -> 259 us (0.87)
  Pallas kernels: 246 us -> 207 us
    pallas_call x1, Pallas kernels: 246 us -> 207 us  [input_gradient(): pl.pallas_call(functools.partial(input_gradient_kernel, n, rows, batches)...]
  transfers between devices with their start and end apart: 1 -> 1, of which waited for: 0 -> 0; matrix products, arithmetic and copies ran while one was open for 1% -> 1% of each run, Pallas kernels for 83% -> 80%
where the time goes in v2:
time: 259 us; the launch traced here: 258 us
  Pallas kernels  207 us (80%)
  blocking collectives  21.6 us (8%)
  between operations  14.1 us (5%)
  matrix products  8.11 us (3%)
  local copies, waits for them, and re-layouts  6.04 us (2%)
    pallas_call x1, Pallas kernels, input_gradient(): pl.pallas_call(functools.partial(input_gradient_kernel, n, rows, batches)...  207 us
    psum x1, blocking collectives, on_device(): gradient_lowrank, projected_rows = lax.psum((low_part, proj_part), 'row')  21.6 us
  transfers between devices with their start and end apart: 1, of which 0 were waited for; matrix products, arithmetic and copies ran while one was open for 1% of the time, Pallas kernels for 80%

profile of v2, /device:TPU:25, one launch (start us, length us, event | category | flops | bytes accessed | tf_op | source)
XLA Modules:
  0.0 258.5 jit_solution(14616036211387694306)
XLA Ops:
  7.2 0.0 copy-start
  7.2 0.0 all-reduce.4.cloned.1.call-start
  7.2 1.1 copy-done
  8.4 0.0 copy-start.1
  8.4 2.3 convolution_bitcast_fusion.1
  10.7 1.6 convolution_bitcast_fusion
  12.2 21.6 %all-reduce = (f32[256,16]{0,1:T(8,128)S(1)}, f32[256,16]{0,1:T(8,128)S(1)}) all-reduce(f32[256,16]{0,1:T(8,128)S(1)} %convolution_bitcast_fusion.1, f32[256,16]{0,1:T(8,128)S(1)} %convolution_bitcast_fusion), channel_id=1, replica_groups=mesh['row'=8,'col'=4] {'row'}, use_global_device_ids=true, to_apply=%region_0.0 | all-reduce | flops 8192 | bytes 65536 | tf_op jit(solution)/shard_map/psum | solution.py:410
  33.8 2.7 %fusion = f32[1856,16]{0,1:T(8,128)} fusion(f32[256,16]{0,1:T(8,128)S(1)} %get-tuple-element.3, bf16[256,1856]{0,1:T(8,128)(2,1)} %param.5), kind=kOutput, calls=%fused_computation.2 | convolution fusion | flops 91255808 | bytes 1085440 | tf_op jit(solution)/shard_map/dot_general | solution.py:411
  36.5 0.0 copy-done.1
  36.5 1.6 convolution_multiply_fusion
  38.1 0.0 all-reduce.4.cloned.1.call-update
  38.1 0.8 pad_maximum_fusion.up3
  38.9 0.9 dynamic-slice_multiply_fusion
  39.8 1.3 copy.9.down3
  41.1 206.9 %input_gradient.1 = bf16[128,3712]{1,0:T(8,128)(2,1)} custom-call(bf16[256,3840]{1,0:T(8,128)(2,1)} %cot_hbm.1, bf16[3712,3840]{1,0:T(8,128)(2,1)} %weight_hbm.1, bf16[48,3840]{1,0:T(8,128)(2,1)} %pad_maximum_fusion.up3, bf16[3712,48]{1,0:T(8,128)(2,1)} %copy.9.down3), custom_call_target="tpu_custom_call" | custom-call | flops 29192355840 | bytes 28508160 | tf_op jit(solution)/shard_map/input_gradient/pallas_call | solution.py:354
  248.0 0.0 all-reduce.4.cloned.1.call-done
  248.0 0.0 copy-start.3
  248.0 0.0 copy-start.2
  248.0 2.2 copy.13
  250.3 0.0 copy-done.3
  250.3 0.6 copy.14
  250.9 0.0 copy-done.2
  250.9 0.7 copy.15
  (2 shorter events, 0.0 us)
Async XLA Ops:
  7.2 1.2 copy-start
  7.2 240.8 %all-reduce.4.cloned.1.call-start = ((), (), s32[]{:S(2)}) async-start(), calls=%async_computation | async-start | bytes 737280 | tf_op jit(solution)/shard_map/psum | solution.py:417
  8.4 28.1 %copy-start.1 = (bf16[256,3840]{1,0:T(8,128)(2,1)S(1)}, bf16[256,3840]{1,0:T(8,128)(2,1)}, u32[]{:S(2)}) copy-start(bf16[256,3840]{1,0:T(8,128)(2,1)} %cot_hbm.1) | copy-start | bytes 5898244
  248.0 2.3 copy-start.3
  248.0 2.9 %copy-start.2 = (f32[16,3840]{1,0:T(8,128)S(1)}, f32[16,3840]{1,0:T(8,128)}, u32[]{:S(2)}) copy-start(f32[16,3840]{1,0:T(8,128)} %get-tuple-element.12) | copy-start | bytes 737284
Sparse Core Ops, SparseCore 0:
  38.2 42.8 all-reduce.3

commit v3 on v2

--- a/solution.py
+++ b/solution.py
@@ -19,10 +19,12 @@
 
 
 def input_gradient_kernel(
-    n, rows, batches, cot_hbm, weight_hbm, up3, down3, out,
+    n, rows, batches, cot_hbm, weight_hbm, up3, down3, inputs, down_rows, out, grad_a, grad_b,
     gathered, weight, part, core_in, half, arrive, fin,
     load_sem, zsend, zrecv, core_send, core_recv, quarter_send, arrive_sem,
     fin_send, fin_recv, credit,
+    small, proj, proj_split, chain, chain_in, small_send, small_recv, proj_send, proj_recv,
+    chain_send, chain_recv, spread_send, spread_recv,
 ):
     z = lax.axis_index("col")
     r = lax.axis_index("row")
@@ -53,19 +55,11 @@
 
     barrier = pltpu.get_barrier_semaphore()
     peers = [partner, x_peer] + [y_peer(k) for k in range(1, ny)]
-    for peer in peers:
+    row_peers = [{"row": (r + k) % rows} for k in range(1, rows)]
+    col_peers = [{"col": (z + k) % n} for k in range(1, n)]
+    for peer in row_peers + col_peers:
         pl.semaphore_signal(barrier, inc=1, device_id=peer, device_id_type=MESH)
-
-    @pl.when(z > 0)
-    def _():
-        pl.semaphore_signal(barrier, inc=1, device_id={"col": z - 1}, device_id_type=MESH)
-
-    @pl.when(z < n - 1)
-    def _():
-        pl.semaphore_signal(barrier, inc=1, device_id={"col": z + 1}, device_id_type=MESH)
-
-    ends = jnp.where(z > 0, 1, 0) + jnp.where(z < n - 1, 1, 0)
-    pl.semaphore_wait(barrier, len(peers) + ends)
+    pl.semaphore_wait(barrier, rows - 1 + n - 1)
     load_own.wait()
 
     def position(holder, s, c):
@@ -228,7 +222,9 @@
     block = min(256, width)
     whole_blocks = width // block
 
-    def multiply(first, count):
+    inner = jnp.logical_and(z > 0, z < n - 1)
+
+    def multiply(first, count, coming):
         size = count * m
         lhs = pl.ds(first * m, size)
         rank = up3.shape[0] // 3
@@ -250,9 +246,14 @@
                 split, down3[pl.ds(start, extent)]
             )
 
-        @pl.loop(0, whole_blocks)
-        def _(j):
-            columns(pl.multiple_of(j * block, block), block)
+        parts = max(1, coming[1])
+        for k in range(parts):
+            if k < coming[1]:
+                pl.when(inner)(functools.partial(receive, coming[0] + k))
+
+            @pl.loop(whole_blocks * k // parts, whole_blocks * (k + 1) // parts)
+            def _(j):
+                columns(pl.multiple_of(j * block, block), block)
 
         if width % block:
             columns(whole_blocks * block, width % block)
@@ -275,15 +276,137 @@
         def _():
             pass_right(s, c)
 
+    rank = up3.shape[0] // 3
+
+    def pieces(value):
+        high = value.astype(jnp.bfloat16)
+        rest = value - high.astype(jnp.float32)
+        middle = rest.astype(jnp.bfloat16)
+        last = (rest - middle.astype(jnp.float32)).astype(jnp.bfloat16)
+        return jnp.concatenate([high, middle, last], axis=0)
+
+    def folded(value):
+        return scaling * (value[:rank] + value[rank : 2 * rank] + value[2 * rank :])
+
+    def small_copy(k):
+        return pltpu.make_async_remote_copy(
+            src_ref=small.at[r], dst_ref=small.at[r],
+            send_sem=small_send.at[k - 1], recv_sem=small_recv.at[r],
+            device_id=row_peers[k - 1], device_id_type=MESH,
+        )
+
+    def proj_copy(k):
+        return pltpu.make_async_remote_copy(
+            src_ref=proj.at[z], dst_ref=proj.at[z],
+            send_sem=proj_send.at[k - 1], recv_sem=proj_recv.at[z],
+            device_id=col_peers[k - 1], device_id_type=MESH,
+        )
+
+    def chain_copy():
+        return pltpu.make_async_remote_copy(
+            src_ref=chain, dst_ref=chain_in,
+            send_sem=chain_send.at[0], recv_sem=chain_recv.at[0],
+            device_id={"col": (z + 1) % n}, device_id_type=MESH,
+        )
+
+    def spread_copy(k):
+        return pltpu.make_async_remote_copy(
+            src_ref=grad_a, dst_ref=grad_a,
+            send_sem=spread_send.at[k - 1], recv_sem=spread_recv.at[0],
+            device_id=col_peers[k - 1], device_id_type=MESH,
+        )
+
+    def send_small():
+        for c in range(chunks):
+            own = pl.ds(c * m, m)
+            small[r, c, pl.ds(0, rank)] = contract_trailing_axis(up3[pl.ds(0, rank)], gathered[own])
+            small[r, c, pl.ds(rank, rank)] = contract_trailing_axis(down_rows[...], inputs[own])
+        for k in range(1, rows):
+            small_copy(k).start()
+
+    def use_small():
+        for k in range(1, rows):
+            other = (r + k) % rows
+            pltpu.make_async_remote_copy(
+                src_ref=small.at[other], dst_ref=small.at[other],
+                send_sem=small_send.at[0], recv_sem=small_recv.at[other],
+                device_id=row_peers[0], device_id_type=MESH,
+            ).wait_recv()
+        for c in range(chunks):
+            value = small[0, c]
+            for q in range(1, rows):
+                value = value + small[q, c]
+            proj[z, c] = value[rank:]
+            term = folded(
+                jnp.dot(
+                    pieces(value[:rank]), inputs[pl.ds(c * m, m)],
+                    preferred_element_type=jnp.float32,
+                )
+            )
+            chain[...] = term if c == 0 else chain[...] + term
+        for k in range(1, n):
+            proj_copy(k).start()
+
+    def advance_chain():
+        @pl.when(z > 0)
+        def _():
+            chain_copy().wait_recv()
+            chain[...] += chain_in[...]
+
+        @pl.when(z < n - 1)
+        def _():
+            chain_copy().start()
+
+        @pl.when(z == n - 1)
+        def _():
+            grad_a[...] = chain[...]
+            for k in range(1, n):
+                spread_copy(k).start()
+
+    def up_gradient():
+        for k in range(1, n):
+            other = (z + k) % n
+            pltpu.make_async_remote_copy(
+                src_ref=proj.at[other], dst_ref=proj.at[other],
+                send_sem=proj_send.at[0], recv_sem=proj_recv.at[other],
+                device_id=col_peers[0], device_id_type=MESH,
+            ).wait_recv()
+
+        @pl.loop(0, total)
+        def _(i):
+            c, _, s, _, _ = place(i)
+            proj_split[i] = pieces(proj[s, c])
+
+        hidden = grad_b.shape[1]
+        step = 384 if hidden % 384 == 0 else hidden
+
+        @pl.loop(0, hidden // step)
+        def _(j):
+            lanes = pl.ds(pl.multiple_of(j * step, 128), step)
+            value = None
+            for i in range(total):
+                term = jnp.dot(
+                    proj_split[i], gathered[pl.ds(i * m, m), lanes],
+                    preferred_element_type=jnp.float32,
+                )
+                value = term if value is None else value + term
+            grad_b[:, lanes] = folded(value)
+
+    send_small()
     previous = None
-    for first, count in batches:
+    for turn, (first, count) in enumerate(batches):
+        coming = batches[turn + 1] if turn + 1 < len(batches) else (0, 0)
         if first >= chunks:
-            pl.loop(first, first + count)(receive)
+
+            @pl.when(jnp.logical_not(inner))
+            def _():
+                pl.loop(first, first + count)(receive)
+
         if previous is not None:
             pl.loop(previous[0], sum(previous))(second_hop)
         if first == 0:
             load_weight.wait()
-        multiply(first, count)
+        multiply(first, count, coming)
         if previous is not None:
             pl.loop(previous[0], sum(previous))(finish)
 
@@ -306,10 +429,31 @@
             half[slot] = part[own] + core_in[slot]
             first_hop(slot, dest)
 
+        if turn == 0:
+            use_small()
+        if turn < chunks:
+            pl.when(z * chunks // n == turn)(advance_chain)
         previous = (first, count)
+
+    up_gradient()
 
     pl.loop(previous[0], sum(previous))(second_hop)
     pl.loop(previous[0], sum(previous))(finish)
+
+    for k in range(1, rows):
+        small_copy(k).wait_send()
+    for k in range(1, n):
+        proj_copy(k).wait_send()
+
+    @pl.when(z < n - 1)
+    def _():
+        chain_copy().wait_send()
+        spread_copy(1).wait_recv()
+
+    @pl.when(z == n - 1)
+    def _():
+        for k in range(1, n):
+            spread_copy(k).wait_send()
 
     for index in range(own_rows // m):
         fin_copy(index * m, index).wait_recv()
@@ -337,7 +481,7 @@
     return tuple(batches)
 
 
-def input_gradient(n, rows, cotangent, weight, up_slice, down_slice):
+def gradients(n, rows, inputs, cotangent, weight, up_slice, down_slice, down_rows):
     shard, hidden = cotangent.shape
     width = weight.shape[0]
     tokens = shard * n
@@ -347,15 +491,21 @@
     own_rows = tokens // rows
     batches = plan(n, shard // m)
     slots = max(count for _, count in batches)
+    rank = up_slice.shape[0]
+    chunks = shard // m
     up3 = jnp.concatenate([up_slice] * 3, axis=0)
     down3 = jnp.concatenate([down_slice * jnp.bfloat16(scaling)] * 3, axis=1)
     vmem = pl.BlockSpec(memory_space=pltpu.VMEM)
     hbm = pl.BlockSpec(memory_space=pl.ANY)
     return pl.pallas_call(
         functools.partial(input_gradient_kernel, n, rows, batches),
-        out_shape=jax.ShapeDtypeStruct((own_rows, width), jnp.bfloat16),
-        in_specs=[hbm, hbm, vmem, vmem],
-        out_specs=vmem,
+        out_shape=[
+            jax.ShapeDtypeStruct((own_rows, width), jnp.bfloat16),
+            jax.ShapeDtypeStruct((rank, inputs.shape[1]), jnp.float32),
+            jax.ShapeDtypeStruct((rank, hidden), jnp.float32),
+        ],
+        in_specs=[hbm, hbm, vmem, vmem, vmem, vmem],
+        out_specs=[vmem, vmem, vmem],
         scratch_shapes=[
             pltpu.VMEM((tokens, hidden), jnp.bfloat16),
             pltpu.VMEM((width, hidden), jnp.bfloat16),
@@ -374,6 +524,19 @@
             pltpu.SemaphoreType.DMA((1,)),
             pltpu.SemaphoreType.DMA((own_rows // m,)),
             pltpu.SemaphoreType.REGULAR((ny + 1,)),
+            pltpu.VMEM((rows, chunks, 2 * rank, m), jnp.float32),
+            pltpu.VMEM((n, chunks, rank, m), jnp.float32),
+            pltpu.VMEM((total, 3 * rank, m), jnp.bfloat16),
+            pltpu.VMEM((rank, inputs.shape[1]), jnp.float32),
+            pltpu.VMEM((rank, inputs.shape[1]), jnp.float32),
+            pltpu.SemaphoreType.DMA((rows - 1,)),
+            pltpu.SemaphoreType.DMA((rows,)),
+            pltpu.SemaphoreType.DMA((n - 1,)),
+            pltpu.SemaphoreType.DMA((n,)),
+            pltpu.SemaphoreType.DMA((1,)),
+            pltpu.SemaphoreType.DMA((1,)),
+            pltpu.SemaphoreType.DMA((n - 1,)),
+            pltpu.SemaphoreType.DMA((1,)),
         ],
         compiler_params=pltpu.CompilerParams(
             collective_id=0, has_side_effects=True, vmem_limit_bytes=62 * 2**20
@@ -384,7 +547,7 @@
             transcendentals=0,
         ),
         name="input_gradient",
-    )(cotangent, weight, up3, down3)
+    )(cotangent, weight, up3, down3, inputs, down_rows.T)
 
 
 def on_device(n, rows, inputs, cotangent, weight, adapter_down_factor, adapter_up_factor):
@@ -402,19 +565,10 @@
     up_weight_slice = lax.dynamic_slice_in_dim(
         adapter_up_factor, row_position * hidden_columns, hidden_columns, 1
     )
-    grad_input = input_gradient(
-        n, rows, cotangent, weight, up_weight_slice, down_factor_columns
-    )
-    low_part = contract_trailing_axis(cotangent, up_weight_slice)
-    proj_part = jnp.dot(inputs, down_factor_rows, preferred_element_type=jnp.float32)
-    gradient_lowrank, projected_rows = lax.psum((low_part, proj_part), "row")
-    part_a = scaling * jnp.dot(
-        inputs.astype(jnp.float32).T, gradient_lowrank, precision=lax.Precision.HIGHEST
-    )
-    part_b = scaling * jnp.dot(
-        projected_rows.T, cotangent.astype(jnp.float32), precision=lax.Precision.HIGHEST
-    )
-    grad_a, grad_b = lax.psum((part_a, part_b), "col")
+    grad_input, grad_a, grad_b = gradients(
+        n, rows, inputs, cotangent, weight, up_weight_slice, down_factor_columns, down_factor_rows
+    )
+    grad_a = grad_a.T
     return (grad_input, grad_a, grad_b)
 
 

time: 259 us -> 234 us (0.903)
  the two profiles are of different devices: /device:TPU:25 before, /device:TPU:17 now
where the time goes in v3:
time: 234 us
  Pallas kernels  221 us (94%)
  local copies, waits for them, and re-layouts  10.6 us (5%)
    pallas_call x1, Pallas kernels, gradients(): pl.pallas_call(functools.partial(input_gradient_kernel, n, rows, batches)...  221 us
    unnamed x6, local copies, waits for them, and re-layouts  7.65 us

profile of v3, /device:TPU:17, one launch (start us, length us, event | category | flops | bytes accessed | tf_op | source)
XLA Modules:
  0.0 234.0 jit_solution(5888983178167858330)
XLA Ops:
  0.6 0.0 copy-start
  0.7 1.6 dynamic-slice_bitcast_fusion.down_rows
  2.3 0.9 dynamic-slice_multiply_fusion
  3.2 0.0 copy-done
  3.3 0.8 pad_maximum_fusion.up3
  4.1 1.3 copy.10.down3
  5.4 2.2 copy.11.inputs
  7.6 221.0 %input_gradient.1 = (bf16[128,3712]{1,0:T(8,128)(2,1)}, f32[16,1856]{1,0:T(8,128)}, f32[16,3840]{1,0:T(8,128)}) custom-call(bf16[256,3840]{1,0:T(8,128)(2,1)} %cot_hbm.1, bf16[3712,3840]{1,0:T(8,128)(2,1)} %weight_hbm.1, bf16[48,3840]{1,0:T(8,128)(2,1)} %pad_maximum_fusion.up3, bf16[3712,48]{1,0:T(8,128)(2,1)} %copy.10.down3, ...), custom_call_target="tpu_custom_call" | custom-call | flops 29192355840 | bytes 28508160 | tf_op jit(solution)/shard_map/input_gradient/pallas_call | solution.py:500
  228.6 2.2 copy.15
  230.8 1.6 copy.16
  232.3 1.7 copy.17
  (2 shorter events, 0.0 us)
Async XLA Ops:
  0.6 2.6 %copy-start = (bf16[16,30720]{1,0:T(8,128)(2,1)S(1)}, bf16[16,30720]{1,0:T(8,128)(2,1)}, u32[]{:S(2)}) copy-start(bf16[16,30720]{1,0:T(8,128)(2,1)} %param.9) | copy-start | bytes 2949124

commit v4 on v2

--- a/solution.py
+++ b/solution.py
@@ -245,10 +245,14 @@
         ).astype(jnp.bfloat16)
 
         def columns(start, extent):
-            value = contract_trailing_axis(gathered[lhs], weight[pl.ds(start, extent)])
-            part[pl.ds(0, size), pl.ds(start, extent)] = value + contract_trailing_axis(
-                split, down3[pl.ds(start, extent)]
-            )
+            for top in range(0, size, 2 * m):
+                height = min(2 * m, size - top)
+                value = contract_trailing_axis(
+                    gathered[pl.ds(first * m + top, height)], weight[pl.ds(start, extent)]
+                )
+                part[pl.ds(top, height), pl.ds(start, extent)] = value + contract_trailing_axis(
+                    split[top : top + height], down3[pl.ds(start, extent)]
+                )
 
         @pl.loop(0, whole_blocks)
         def _(j):

time: 259 us -> 278 us (1.073)
  Pallas kernels: 207 us -> 224 us
    pallas_call x1, Pallas kernels: 207 us -> 224 us  [input_gradient(): pl.pallas_call(functools.partial(input_gradient_kernel, n, rows, batches)...]
  transfers between devices with their start and end apart: 1 -> 1, of which waited for: 0 -> 0; matrix products, arithmetic and copies ran while one was open for 1% -> 1% of each run, Pallas kernels for 80% -> 81%
where the time goes in v4:
time: 278 us; the launch traced here: 276 us
  Pallas kernels  224 us (81%)
  blocking collectives  21.6 us (8%)
  between operations  14.1 us (5%)
  matrix products  8.11 us (3%)
  local copies, waits for them, and re-layouts  6.04 us (2%)
    pallas_call x1, Pallas kernels, input_gradient(): pl.pallas_call(functools.partial(input_gradient_kernel, n, rows, batches)...  224 us
    psum x1, blocking collectives, on_device(): gradient_lowrank, projected_rows = lax.psum((low_part, proj_part), 'row')  21.6 us
  transfers between devices with their start and end apart: 1, of which 0 were waited for; matrix products, arithmetic and copies ran while one was open for 1% of the time, Pallas kernels for 81%

profile of v4, /device:TPU:25, one launch (start us, length us, event | category | flops | bytes accessed | tf_op | source)
XLA Modules:
  0.0 276.0 jit_solution(14814373194174172761)
XLA Ops:
  7.2 0.0 copy-start
  7.2 0.0 all-reduce.4.cloned.1.call-start
  7.2 1.1 copy-done
  8.4 0.0 copy-start.1
  8.4 2.3 convolution_bitcast_fusion.1
  10.7 1.6 convolution_bitcast_fusion
  12.2 21.6 %all-reduce = (f32[256,16]{0,1:T(8,128)S(1)}, f32[256,16]{0,1:T(8,128)S(1)}) all-reduce(f32[256,16]{0,1:T(8,128)S(1)} %convolution_bitcast_fusion.1, f32[256,16]{0,1:T(8,128)S(1)} %convolution_bitcast_fusion), channel_id=1, replica_groups=mesh['row'=8,'col'=4] {'row'}, use_global_device_ids=true, to_apply=%region_0.0 | all-reduce | flops 8192 | bytes 65536 | tf_op jit(solution)/shard_map/psum | solution.py:414
  33.8 2.7 fusion
  36.5 0.0 copy-done.1
  36.5 1.6 convolution_multiply_fusion
  38.1 0.0 all-reduce.4.cloned.1.call-update
  38.1 0.8 pad_maximum_fusion.up3
  38.9 0.9 dynamic-slice_multiply_fusion
  39.8 1.3 copy.9.down3
  41.1 224.4 %input_gradient.1 = bf16[128,3712]{1,0:T(8,128)(2,1)} custom-call(bf16[256,3840]{1,0:T(8,128)(2,1)} %cot_hbm.1, bf16[3712,3840]{1,0:T(8,128)(2,1)} %weight_hbm.1, bf16[48,3840]{1,0:T(8,128)(2,1)} %pad_maximum_fusion.up3, bf16[3712,48]{1,0:T(8,128)(2,1)} %copy.9.down3), custom_call_target="tpu_custom_call" | custom-call | flops 29192355840 | bytes 28508160 | tf_op jit(solution)/shard_map/input_gradient/pallas_call | solution.py:358
  265.5 0.0 all-reduce.4.cloned.1.call-done
  265.5 0.0 copy-start.3
  265.5 0.0 copy-start.2
  265.5 2.2 copy.13
  267.8 0.0 copy-done.3
  267.8 0.6 copy.14
  268.4 0.0 copy-done.2
  268.4 0.7 copy.15
  (2 shorter events, 0.0 us)
Async XLA Ops:
  7.2 1.2 copy-start
  7.2 258.3 %all-reduce.4.cloned.1.call-start = ((), (), s32[]{:S(2)}) async-start(), calls=%async_computation | async-start | bytes 737280 | tf_op jit(solution)/shard_map/psum | solution.py:421
  8.4 28.1 %copy-start.1 = (bf16[256,3840]{1,0:T(8,128)(2,1)S(1)}, bf16[256,3840]{1,0:T(8,128)(2,1)}, u32[]{:S(2)}) copy-start(bf16[256,3840]{1,0:T(8,128)(2,1)} %cot_hbm.1) | copy-start | bytes 5898244
  265.5 2.3 copy-start.3
  265.5 2.9 %copy-start.2 = (f32[16,3840]{1,0:T(8,128)S(1)}, f32[16,3840]{1,0:T(8,128)}, u32[]{:S(2)}) copy-start(f32[16,3840]{1,0:T(8,128)} %get-tuple-element.12) | copy-start | bytes 737284
Sparse Core Ops, SparseCore 0:
  38.2 42.4 all-reduce.3
